TPU v7x, 32 devices: a whole 2x2x4 slice. The times are simulated.
32 devices in a mesh: groups: 2 (over y), context: 2 (over x), expert: 4 (over z), tensor: 2 (over core).
Axes of the slice: x: 2, y: 2, z: 4, core: 2. Of those that a mesh axis runs over, the one named last changes fastest.
Arguments:
- queries: bfloat16 [2048, 2048], P(('groups', 'context', 'expert'), 'tensor'), parts along dimension 0, may hold values from -60 to 60
- keys: bfloat16 [2048, 512], P(('groups', 'context', 'expert'), 'tensor'), parts along dimension 0, may hold values from -5 to 5
- values: bfloat16 [2048, 512], P(('groups', 'context', 'expert'), 'tensor'), parts along dimension 0, may hold values from -6 to 6
- resid: bfloat16 [2048, 2048], P(('groups', 'context', 'expert'), 'tensor'), parts along dimension 0, may hold values from -200 to 200
- expert_out: bfloat16 [4, 4, 4, 80, 2048], P(('groups', 'context'), 'expert', None, None, 'tensor'), parts along dimension 0, may hold values from -6 to 6
- routes: int32 [2048, 2], P(('groups', 'context', 'expert')), parts along dimension 0, may hold values from 0 to 3, all different within a row; in each aligned block of 128 rows (0 to 127, 128 to 255, ...) at most 80 rows name the same one
- route_weights: float32 [2048, 2], P(('groups', 'context', 'expert')), parts along dimension 0, may hold values from 0.1 to 1
- pattern: int32 [8, 8], P(('context', 'expert')), may hold values from 0 to 1, as said below
- lengths: int32 [128], P('groups'), parts along dimension 0, may hold values from 1 to 256, 1024 in all
- teacher: float32 [128, 64], P('groups'), parts along dimension 0, may hold values from 0 to 1
- gain: float32 [2048], P('tensor'), may hold values from 0.5 to 1.5
- head_weight: float32 [2048, 64], P('tensor'), may hold values from -0.125 to 0.125
Outputs:
- grad_query: bfloat16 [2048, 2048], P(('groups', 'context', 'expert'), 'tensor'), parts along dimension 0
- grad_key: float32 [2048, 512], P(('groups', 'context', 'expert'), 'tensor'), parts along dimension 0
- value_gradient: float32 [2048, 512], P(('groups', 'context', 'expert'), 'tensor'), parts along dimension 0
- grad_expert: bfloat16 [4, 4, 4, 80, 2048], P(('groups', 'context'), 'expert', None, None, 'tensor'), parts along dimension 0
There are 2 independent parts, one for each index of `groups`. A program takes and returns all parts, laid end to end along the dimension named above; an argument that names none is the same for every part. Nothing has to cross between parts.
Inputs may be any that keep to these rules, and one draw needn't show every extreme that they name: `pattern`: entry (i, i) is 1; entry (i, j) for i != j is 0 unless i XOR j is a power of two. `routes`: each row names 2 different experts; at most 80 of the pairs of the rows of one device name one expert.
All inputs are finite; a program needn't handle non-finite values.
Results may differ from a plain program's by a relative error of at most 0.0058.
Values may be sent and summed in bfloat16 or wider, within the bound.
A program may use at most 64 MiB of HBM per device.

v0:
```python
import jax
import jax.numpy as jnp
from jax import lax
from jax.sharding import PartitionSpec as P

BLOCK_POSITIONS = 128
HEAD_FEATURES = 128
LOSS_SCALE = 256
D = 2048
EPSILON = 1e-05
NEGATIVE = -1e30
HIGHEST_PRECISION = lax.Precision.HIGHEST


def swapped(array, axis, distance):
    return lax.ppermute(array, axis, [(i, i ^ 1 << distance) for i in range(lax.axis_size(axis))])


def block_probs(query_block, key_set, key_keep, score_scale):
    scores = (
        jnp.einsum("qkgd,skd->kgqs", query_block, key_set, preferred_element_type=jnp.float32)
        * score_scale
    )
    scores = jnp.where(key_keep[None, None, None, :], scores, NEGATIVE)
    row_max = jnp.max(scores, axis=-1, keepdims=True)
    raised = jnp.exp(scores - row_max)
    return raised / jnp.sum(raised, axis=-1, keepdims=True)


def local(
    queries,
    keys,
    values,
    resid,
    expert_out,
    routes,
    route_weights,
    pattern,
    lengths,
    teacher,
    gain,
    head_weight,
):
    shard_bits = lax.axis_size(("context", "expert")).bit_length() - 1
    shard_id = lax.axis_index(("context", "expert"))
    tok_dev = queries.shape[0]
    blocks = tok_dev // BLOCK_POSITIONS
    device_levels = blocks.bit_length() - 1
    kv_dev = keys.shape[1] // HEAD_FEATURES
    heads_dev = queries.shape[1] // HEAD_FEATURES
    group_size = heads_dev // kv_dev
    row_width = queries.shape[1]
    kv_width = keys.shape[1]
    score_scale = HEAD_FEATURES ** (-0.5)
    q_blocks = queries.reshape(blocks, BLOCK_POSITIONS, kv_dev, group_size, HEAD_FEATURES)
    key_rows = keys.reshape(blocks, BLOCK_POSITIONS, kv_width)
    value_rows = values.reshape(blocks, BLOCK_POSITIONS, kv_width)
    received = [
        swapped((keys, values), ("context", "expert"), level_bit) for level_bit in range(shard_bits)
    ]

    def key_value_sets(partner_pairs, block_position):
        key_list = [key_rows[block_position]] + [
            key_rows[block_position ^ 1 << level] for level in range(device_levels)
        ]
        value_list = [value_rows[block_position]] + [
            value_rows[block_position ^ 1 << level] for level in range(device_levels)
        ]
        key_list = key_list + [
            pair[0].reshape(blocks, BLOCK_POSITIONS, kv_width)[block_position]
            for pair in partner_pairs
        ]
        value_list = value_list + [
            pair[1].reshape(blocks, BLOCK_POSITIONS, kv_width)[block_position]
            for pair in partner_pairs
        ]
        key_set = jnp.concatenate(key_list, axis=0).reshape(-1, kv_dev, HEAD_FEATURES)
        value_set = jnp.concatenate(value_list, axis=0).reshape(-1, kv_dev, HEAD_FEATURES)
        return (key_set, value_set)

    def block_flags(block_position):
        partners = [
            shard_id * blocks + (block_position ^ 1 << level) for level in range(device_levels)
        ]
        partners = partners + [
            jnp.bitwise_xor(shard_id, 1 << level_bit) * blocks + block_position
            for level_bit in range(shard_bits)
        ]
        flag_bits = jnp.stack(
            [jnp.int32(1)] + [pattern[block_position, partner] for partner in partners]
        )
        return jnp.repeat(flag_bits, BLOCK_POSITIONS) > 0

    block_position = 0
    key_set, value_set = key_value_sets(received, block_position)
    attn_prob = block_probs(
        q_blocks[block_position], key_set, block_flags(block_position), score_scale
    )
    prob_list = [attn_prob]
    block_out = jnp.einsum(
        "kgqs,skd->qkgd",
        attn_prob.astype(jnp.bfloat16),
        value_set,
        preferred_element_type=jnp.float32,
    )
    attn_list = block_out.reshape(BLOCK_POSITIONS, row_width)
    experts = expert_out.shape[2]
    capacity = expert_out.shape[3]
    arrived = lax.all_to_all(expert_out, "expert", split_axis=2, concat_axis=1, tiled=True)
    flat_rows = arrived.reshape(experts * capacity, -1)
    pair_routes = routes.reshape(-1)
    onehot = (pair_routes[:, None] == jnp.arange(experts, dtype=jnp.int32)[None, :]).astype(
        jnp.int32
    )
    slot_rank = jnp.sum((jnp.cumsum(onehot, axis=0) - onehot) * onehot, axis=1)
    flat_index = pair_routes * capacity + slot_rank
    picked = (
        jnp.take(flat_rows, flat_index, axis=0)
        .astype(jnp.float32)
        .reshape(tok_dev, routes.shape[1], -1)
    )
    mixture = jnp.sum(route_weights[:, :, None] * picked, axis=1)
    hidden = resid.astype(jnp.float32) + attn_list + mixture
    square_sum = lax.psum(jnp.sum(hidden * hidden, axis=1), "tensor")
    row_rms = jnp.sqrt(square_sum / D + EPSILON)
    normed = hidden / row_rms[:, None] * gain
    logits = lax.psum(jnp.dot(normed, head_weight, precision=HIGHEST_PRECISION), "tensor")
    turn_ends = jnp.cumsum(lengths)
    position = shard_id * tok_dev + jnp.arange(tok_dev, dtype=jnp.int32)
    turn_id = jnp.sum((turn_ends[None, :] <= position[:, None]).astype(jnp.int32), axis=1)
    turn_pick = (turn_id[:, None] == jnp.arange(lengths.shape[0], dtype=jnp.int32)[None, :]).astype(
        jnp.float32
    )
    target = jnp.dot(turn_pick, teacher, precision=HIGHEST_PRECISION)
    grad_logit = (jax.nn.sigmoid(logits) - target) * LOSS_SCALE
    grad_normed = jnp.dot(grad_logit, head_weight.T, precision=HIGHEST_PRECISION)
    inner_sum = lax.psum(jnp.sum(grad_normed * gain * hidden, axis=1), "tensor")
    grad_hidden = (
        gain * grad_normed / row_rms[:, None] - hidden * (inner_sum / (D * row_rms**3))[:, None]
    )
    grad_out = grad_hidden.astype(jnp.bfloat16).reshape(
        blocks, BLOCK_POSITIONS, kv_dev, group_size, HEAD_FEATURES
    )
    own_key = jnp.zeros((blocks, BLOCK_POSITIONS, kv_width), jnp.float32)
    local_value = jnp.zeros((blocks, BLOCK_POSITIONS, kv_width), jnp.float32)
    send_key = [[] for level_bit in range(shard_bits)]
    outgoing_value = [[] for level_bit in range(shard_bits)]
    block_position = 0
    key_set, value_set = key_value_sets(received, block_position)
    attn_prob = prob_list[block_position]
    weight_rows = attn_prob.astype(jnp.bfloat16)
    grad_prob = jnp.einsum(
        "qkgd,skd->kgqs", grad_out[block_position], value_set, preferred_element_type=jnp.float32
    )
    value_set_gradient = jnp.einsum(
        "rcnw,nrco->wro", weight_rows, grad_out[block_position], preferred_element_type=jnp.float32
    ).reshape(-1, BLOCK_POSITIONS, kv_width)
    row_delta = jnp.sum(attn_prob * grad_prob, axis=-1, keepdims=True)
    grad_score = (attn_prob * (grad_prob - row_delta) * score_scale).astype(jnp.bfloat16)
    grad_query = jnp.einsum(
        "kgqs,skd->qkgd", grad_score, key_set, preferred_element_type=jnp.float32
    )
    grad_rows = grad_query.reshape(BLOCK_POSITIONS, row_width).astype(jnp.bfloat16)
    grad_kset = jnp.einsum(
        "rcnw,nrco->wro", grad_score, q_blocks[block_position], preferred_element_type=jnp.float32
    ).reshape(-1, BLOCK_POSITIONS, kv_width)
    own_key = own_key.at[block_position].add(grad_kset[0])
    local_value = local_value.at[block_position].add(value_set_gradient[0])
    for level_bit in range(shard_bits):
        send_key[level_bit].append(grad_kset[1 + device_levels + level_bit])
        outgoing_value[level_bit].append(value_set_gradient[1 + device_levels + level_bit])
    for level_bit in range(shard_bits):
        back_key, back_value = (
            swapped(
                jnp.stack(send_key[level_bit]).astype(jnp.bfloat16),
                ("context", "expert"),
                level_bit,
            ).astype(jnp.float32),
            swapped(
                jnp.stack(outgoing_value[level_bit]).astype(jnp.bfloat16),
                ("context", "expert"),
                level_bit,
            ).astype(jnp.float32),
        )
        own_key = own_key + back_key
        local_value = local_value + back_value
    contrib = (
        (route_weights[:, :, None] * grad_hidden[:, None, :])
        .astype(jnp.bfloat16)
        .reshape(-1, grad_hidden.shape[1])
    )
    buffer = (
        jnp.zeros((experts * capacity, grad_hidden.shape[1]), jnp.bfloat16)
        .at[flat_index]
        .set(contrib)
    )
    grad_expert = lax.all_to_all(
        buffer.reshape(1, experts, 1, capacity, -1),
        "expert",
        split_axis=1,
        concat_axis=2,
        tiled=True,
    )
    return (
        grad_rows,
        own_key.reshape(tok_dev, kv_width),
        local_value.reshape(tok_dev, kv_width),
        grad_expert,
    )


def solution(mesh):
    placed = (
        P(("groups", "context", "expert"), "tensor"),
        P(("groups", "context", "expert"), "tensor"),
        P(("groups", "context", "expert"), "tensor"),
        P(("groups", "context", "expert"), "tensor"),
        P(("groups", "context"), "expert", None, None, "tensor"),
        P(("groups", "context", "expert"), None),
        P(("groups", "context", "expert"), None),
        P(("context", "expert"), None),
        P("groups"),
        P("groups", None),
        P("tensor"),
        P("tensor", None),
    )
    return jax.shard_map(
        local,
        mesh=mesh,
        in_specs=placed,
        out_specs=(
            P(("groups", "context", "expert"), "tensor"),
            P(("groups", "context", "expert"), "tensor"),
            P(("groups", "context", "expert"), "tensor"),
            P(("groups", "context"), "expert", None, None, "tensor"),
        ),
        check_vma=False,
    )
```

profile of v0, /device:TPU:0, one launch (start us, length us, event | category | flops | bytes accessed | tf_op | source)
XLA Modules:
  0.0 86.3 jit_solution(17052111443029709541)
XLA Ops:
  0.7 1.0 %copy.146 = bf16[128,256]{0,1:T(8,128)(2,1)S(1)} copy(bf16[128,256]{1,0:T(8,128)(2,1)} %param.17) | data formatting | bytes 131072 | tf_op args[1]
  1.7 3.0 %collective-permute-start.2 = (bf16[128,256]{0,1:T(8,128)(2,1)S(1)}, bf16[128,256]{0,1:T(8,128)(2,1)S(1)}, u32[]{:S(2)}, u32[]{:S(2)}) collective-permute-start(bf16[128,256]{0,1:T(8,128)(2,1)S(1)} %copy.146), channel_id=1, source_target_pairs={{0,8},{2,10},{4,12},{6,14},{8,0},{10,2},{12,4},{14,6},{1,9},{3,11}... | collective-permute-start | bytes 196616 | tf_op jit(solution)/shard_map/ppermute | solution.py:16
  4.7 2.6 %collective-permute-start.1 = (bf16[128,256]{0,1:T(8,128)(2,1)S(1)}, bf16[128,256]{0,1:T(8,128)(2,1)S(1)}, u32[]{:S(2)}, u32[]{:S(2)}) collective-permute-start(bf16[128,256]{0,1:T(8,128)(2,1)S(1)} %copy.146), channel_id=1, source_target_pairs={{0,4},{2,6},{4,0},{6,2},{8,12},{10,14},{12,8},{14,10},{1,5},{3,7},... | collective-permute-start | bytes 196616 | tf_op jit(solution)/shard_map/ppermute | solution.py:16
  7.6 1.6 %collective-permute-start.3 = (bf16[128,256]{1,0:T(8,128)(2,1)}, bf16[128,256]{1,0:T(8,128)(2,1)S(1)}, u32[]{:S(2)}, u32[]{:S(2)}) collective-permute-start(bf16[128,256]{1,0:T(8,128)(2,1)} %param.18), channel_id=1, source_target_pairs={{0,2},{2,0},{4,6},{6,4},{8,10},{10,8},{12,14},{14,12},{1,3},{3,1},... | collective-permute-start | bytes 196616 | tf_op jit(solution)/shard_map/ppermute | solution.py:16
  9.7 3.9 %all-to-all-start = ((bf16[1,1,4,80,1024]{4,3,1,0,2:T(8,128)(2,1)}), bf16[1,1,4,80,1024]{4,3,1,0,2:T(8,128)(2,1)S(1)}, u32[]{:S(2)}, u32[]{:S(2)}) async-start(bf16[1,1,4,80,1024]{4,3,1,0,2:T(8,128)(2,1)} %bitcast.132), calls=%async_computation | async-start | bytes 1310720 | tf_op jit(solution)/shard_map/all_to_all | solution.py:109
  15.4 1.4 %constant_dynamic-slice_fusion.2 = (s32[1,1]{1,0:T(1,128)}, s32[1,1]{1,0:T(1,128)}, s32[1,1]{1,0:T(1,128)}) fusion(s32[1,8]{1,0:T(1,128)} %param.23, s32[]{:T(128)S(6)} %select_n.39, s32[]{:T(128)S(6)} %select_n.41, s32[]{:T(128)S(6)} %select_n.40), kind=kLoop, calls=%fused_computation.66 | loop fusion | bytes 36 | tf_op jit(solution)/shard_map/dynamic_slice | solution.py:90
  16.7 2.0 %add_compare_fusion = pred[4]{0:T(512)(128)(4,1)S(1)} fusion(s32[1]{0:T(128)} %bitcast.5, s32[1]{0:T(128)} %bitcast.4, s32[1]{0:T(128)} %bitcast.3, s32[1]{0:T(128)} %constant.90.clone.1), kind=kLoop, calls=%fused_computation.69 | loop fusion | flops 16 | bytes 20 | tf_op jit(solution)/shard_map/gt | solution.py:92
  21.0 1.2 %reduce-window.18 = s32[4,2,128]{2,1,0:T(2,128)S(1)} reduce-window(s32[4,2,128]{2,1,0:T(2,128)S(1)} %compare_convert_fusion, s32[]{:T(128)} %constant.91.clone.1), window={size=1x1x128 pad=0_0x0_0x127_0}, to_apply=%region_2.3 | reduce-window | flops 130048 | bytes 8196 | tf_op jit(solution)/shard_map/reduce-window
  23.3 2.1 %collective-permute-start = (bf16[128,256]{0,1:T(8,128)(2,1)S(1)}, bf16[128,256]{0,1:T(8,128)(2,1)S(1)}, u32[]{:S(2)}, u32[]{:S(2)}) collective-permute-start(bf16[128,256]{0,1:T(8,128)(2,1)S(1)} %copy.146), channel_id=1, source_target_pairs={{0,2},{2,0},{4,6},{6,4},{8,10},{10,8},{12,14},{14,12},{1,3},{3,1},... | collective-permute-start | bytes 196616 | tf_op jit(solution)/shard_map/ppermute | solution.py:16
  25.6 4.2 %collective-permute-done = bf16[128,256]{0,1:T(8,128)(2,1)S(1)} collective-permute-done((bf16[128,256]{0,1:T(8,128)(2,1)S(1)}, bf16[128,256]{0,1:T(8,128)(2,1)S(1)}, u32[]{:S(2)}, u32[]{:S(2)}) %collective-permute-start) | collective-permute-done | bytes 65568 | tf_op jit(solution)/shard_map/ppermute | solution.py:16
  29.8 2.2 %fusion.42 = (f32[2,4,128]{2,1,0:T(4,128)S(1)}, f32[2,4,128,512]{2,3,1,0:T(8,128)}) fusion(pred[512]{0:T(512)(128)(4,1)S(1)} %broadcast_bitcast_fusion, bf16[512,2,128,1]{0,2,3,1:T(8,128)(2,1)S(1)} %bitcast.138, bf16[128,2,4,128]{0,3,2,1:T(8,128)(2,1)S(1)} %bitcast.136), kind=kOutput, calls=%fused_computation.82 | convolution fusion | flops 136315392 | bytes 2626048 | tf_op jit(solution)/shard_map/sub | solution.py:26
  32.0 1.9 %fusion.20 = f32[2,128,4,128]{3,1,2,0:T(8,128)S(1)} fusion(bf16[512,2,128,1]{0,2,3,1:T(8,128)(2,1)S(1)} %bitcast.128, f32[2,4,128,512]{2,3,1,0:T(8,128)} %get-tuple-element.62, f32[2,4,128]{2,1,0:T(4,128)S(1)} %get-tuple-element.61), kind=kOutput, calls=%fused_computation.38 | convolution fusion | flops 135266304 | bytes 2887680 | tf_op jit(solution)/shard_map/kgqs,skd->qkgd/dot_general | solution.py:100
  34.2 1.2 %gather_fusion = bf16[256,1024]{1,0:T(8,128)(2,1)S(1)} fusion(bf16[320,1024]{1,0:T(8,128)(2,1)S(1)} %bitcast.126, s32[1024]{0:T(1024)S(1)} %pad_clamp_fusion), kind=kCustom, calls=%fused_computation | custom fusion | bytes 1049600 | tf_op jit(solution)/shard_map/jit(_take)/gather | solution.py:118
  35.6 1.7 %multiply_reduce_fusion = f32[128,1024]{1,0:T(8,128)S(1)} fusion(bf16[128,2,1024]{2,1,0:T(2,128)(2,1)S(1)} %gather.7, pred[128,2]{1,0:T(8,128)(4,1)S(1)} %copy.158, f32[128,2]{1,0:T(8,128)S(1)} %copy.152), kind=kLoop, calls=%fused_computation.21 | loop fusion | flops 917504 | bytes 1049856 | tf_op jit(solution)/shard_map/reduce_sum | solution.py:122
  37.4 2.5 %psum.21 = f32[128]{0:T(128)S(1)} all-reduce(f32[128]{0:T(128)S(1)} %get-tuple-element.50), channel_id=1, replica_groups=mesh['groups'=2,'context'=2,'expert'=4,'tensor'=2] {'tensor'}, use_global_device_ids=true, to_apply=%region_7.8 | all-reduce | flops 128 | bytes 1024 | tf_op jit(solution)/shard_map/psum | solution.py:124
  40.7 3.4 %psum.22 = f32[128,64]{0,1:T(8,128)S(1)} all-reduce(f32[128,64]{0,1:T(8,128)S(1)} %fusion.16), channel_id=1, replica_groups=mesh['groups'=2,'context'=2,'expert'=4,'tensor'=2] {'tensor'}, use_global_device_ids=true, to_apply=%region_8.9 | all-reduce | flops 8192 | bytes 65536 | tf_op jit(solution)/shard_map/psum | solution.py:127
  45.1 2.5 %psum.23 = f32[128]{0:T(128)S(1)} all-reduce(f32[128]{0:T(128)S(1)} %get-tuple-element.63), channel_id=1, replica_groups=mesh['groups'=2,'context'=2,'expert'=4,'tensor'=2] {'tensor'}, use_global_device_ids=true, to_apply=%region_12.13 | all-reduce | flops 128 | bytes 1024 | tf_op jit(solution)/shard_map/psum | solution.py:137
  47.9 2.9 %fusion.44 = (bf16[512,2,128]{0,2,1:T(8,128)(2,1)S(1)}, f32[512,2,128]{0,2,1:T(8,128)}) fusion(bf16[128,2,4,128]{0,3,2,1:T(8,128)(2,1)S(1)} %bitcast.130, f32[2,4,128,512]{2,3,1,0:T(8,128)} %get-tuple-element.62, f32[2,4,128]{2,1,0:T(4,128)S(1)} %get-tuple-element.61), kind=kOutput, calls=%fused_computation.84 | convolution fusion | flops 135397376 | bytes 3149824 | tf_op jit(solution)/shard_map/rcnw,nrco->wro/dot_general | solution.py:155
  50.8 1.8 %fusion.45 = f32[2,512,128,4]{2,1,3,0:T(8,128)} fusion(bf16[512,2,128,1]{0,2,3,1:T(8,128)(2,1)S(1)} %bitcast.129, bf16[128,2,4,128]{0,3,2,1:T(8,128)(2,1)S(1)} %bitcast.131), kind=kOutput, calls=%fused_computation.85 | convolution fusion | flops 134217728 | bytes 2621440 | tf_op jit(solution)/shard_map/qkgd,skd->kgqs/dot_general | solution.py:152
  52.9 0.8 collective-permute-start.10
  53.8 1.5 %collective-permute-start.11 = (bf16[1,128,256]{2,1,0:T(8,128)(2,1)S(1)}, bf16[1,128,256]{2,1,0:T(8,128)(2,1)S(1)}, u32[]{:S(2)}, u32[]{:S(2)}) collective-permute-start(bf16[1,128,256]{2,1,0:T(8,128)(2,1)S(1)} %copy.176), channel_id=1, source_target_pairs={{0,8},{2,10},{4,12},{6,14},{8,0},{10,2},{12,4},{14,6},{1,9},{3,11}... | collective-permute-start | bytes 196616 | tf_op jit(solution)/shard_map/ppermute | solution.py:16
  55.3 1.6 %collective-permute-start.9 = (bf16[1,128,256]{2,1,0:T(8,128)(2,1)S(1)}, bf16[1,128,256]{2,1,0:T(8,128)(2,1)S(1)}, u32[]{:S(2)}, u32[]{:S(2)}) collective-permute-start(bf16[1,128,256]{2,1,0:T(8,128)(2,1)S(1)} %copy.173), channel_id=1, source_target_pairs={{0,2},{2,0},{4,6},{6,4},{8,10},{10,8},{12,14},{14,12},{1,3},{3,1},... | collective-permute-start | bytes 196616 | tf_op jit(solution)/shard_map/ppermute | solution.py:16
  58.0 2.6 %scatter_custom_fusion = bf16[320,1024]{1,0:T(8,128)(2,1)} fusion(s32[256]{0:T(256)S(1)} %bitcast.149, f32[256,1024]{1,0:T(8,128)S(1)} %mul.133, f32[256]{0:T(256)S(1)} %mul.130, bf16[]{:T(256)} %constant.112.clone.1), kind=kCustom, calls=%fused_computation.28 | custom fusion | flops 524288 | bytes 1704962 | tf_op jit(solution)/shard_map/scatter | solution.py:195
  60.6 3.5 %all-to-all-start.1 = ((bf16[1,4,1,80,1024]{4,3,2,0,1:T(8,128)(2,1)}), bf16[1,4,1,80,1024]{4,3,2,0,1:T(8,128)(2,1)S(1)}, u32[]{:S(2)}, u32[]{:S(2)}) async-start(bf16[1,4,1,80,1024]{4,3,2,0,1:T(8,128)(2,1)} %bitcast.43), calls=%async_computation.1 | async-start | bytes 1310720 | tf_op jit(solution)/shard_map/all_to_all | solution.py:197
  64.1 4.2 %convolution_convert_fusion = bf16[2,128,4,128]{3,1,2,0:T(8,128)(2,1)S(1)} fusion(bf16[512,2,128,1]{0,2,3,1:T(8,128)(2,1)S(1)} %bitcast.139, f32[2,512,128,4]{2,1,3,0:T(8,128)} %fusion.45, f32[2,4,128,512]{2,3,1,0:T(8,128)} %get-tuple-element.62, f32[2,4,128]{2,1,0:T(4,128)S(1)} %get-tuple-element.61), kind=kOutput, calls=%fused_computation.17 | convolution fusion | flops 138020352 | bytes 4722688 | tf_op jit(solution)/shard_map/kgqs,skd->qkgd/dot_general | solution.py:160
  68.3 4.2 %fusion.43 = (bf16[512,2,128]{0,2,1:T(8,128)(2,1)S(1)}, f32[512,2,128]{0,2,1:T(8,128)S(1)}) fusion(bf16[128,2,4,128]{0,3,2,1:T(8,128)(2,1)S(1)} %bitcast.137, f32[2,512,128,4]{2,1,3,0:T(8,128)} %fusion.45, f32[2,4,128,512]{2,3,1,0:T(8,128)} %get-tuple-element.62, f32[2,4,128]{2,1,0:T(4,128)S(1)} %get-tuple-element.61), kind=kOutput, calls=%fused_computation.83 | convolution fusion | flops 138020352 | bytes 5246976 | tf_op jit(solution)/shard_map/rcnw,nrco->wro/dot_general | solution.py:164
  72.6 0.9 %slice.99 = f32[128,2,128]{0,2,1:T(8,128)S(1)} slice(f32[512,2,128]{0,2,1:T(8,128)} %get-tuple-element.68), slice={[0:128], [0:2], [0:128]} | slice | bytes 262144 | tf_op jit(solution)/shard_map/slice | solution.py:168
  73.9 0.9 copy.178
  74.8 3.0 %collective-permute-start.7 = (bf16[1,128,256]{2,1,0:T(8,128)(2,1)S(1)}, bf16[1,128,256]{2,1,0:T(8,128)(2,1)S(1)}, u32[]{:S(2)}, u32[]{:S(2)}) collective-permute-start(bf16[1,128,256]{2,1,0:T(8,128)(2,1)S(1)} %copy.169), channel_id=1, source_target_pairs={{0,4},{2,6},{4,0},{6,2},{8,12},{10,14},{12,8},{14,10},{1,5},{3,7},... | collective-permute-start | bytes 196616 | tf_op jit(solution)/shard_map/ppermute | solution.py:16
  78.4 1.5 %collective-permute-start.6 = (bf16[1,128,256]{2,1,0:T(8,128)(2,1)S(1)}, bf16[1,128,256]{2,1,0:T(8,128)(2,1)S(1)}, u32[]{:S(2)}, u32[]{:S(2)}) collective-permute-start(bf16[1,128,256]{2,1,0:T(8,128)(2,1)S(1)} %copy.167), channel_id=1, source_target_pairs={{0,2},{2,0},{4,6},{6,4},{8,10},{10,8},{12,14},{14,12},{1,3},{3,1},... | collective-permute-start | bytes 196616 | tf_op jit(solution)/shard_map/ppermute | solution.py:16
  80.7 3.5 %collective-permute-done.7 = bf16[1,128,256]{2,1,0:T(8,128)(2,1)S(1)} collective-permute-done((bf16[1,128,256]{2,1,0:T(8,128)(2,1)S(1)}, bf16[1,128,256]{2,1,0:T(8,128)(2,1)S(1)}, u32[]{:S(2)}, u32[]{:S(2)}) %collective-permute-start.7) | collective-permute-done | bytes 65568 | tf_op jit(solution)/shard_map/ppermute | solution.py:16
  85.5 0.8 copy.198
  (86 shorter events, 13.3 us)
Async XLA Ops:
  0.6 39.3 %copy-start = (f32[1024,64]{0,1:T(8,128)S(1)}, f32[1024,64]{0,1:T(8,128)}, u32[]{:S(2)}) copy-start(f32[1024,64]{0,1:T(8,128)} %param.27) | copy-start | bytes 786436
  0.6 24.8 %copy-start.3 = (bf16[128,256]{1,0:T(8,128)(2,1)S(1)}, bf16[128,256]{1,0:T(8,128)(2,1)}, u32[]{:S(2)}) copy-start(bf16[128,256]{1,0:T(8,128)(2,1)} %param.18) | copy-start | bytes 196612
  0.7 22.2 %copy-start.4 = (s32[128,2]{0,1:T(2,128)S(1)}, s32[128,2]{0,1:T(2,128)}, u32[]{:S(2)}) copy-start(s32[128,2]{0,1:T(2,128)} %param.21) | copy-start | bytes 3076
  0.7 22.3 %copy-start.1 = (bf16[128,1024]{1,0:T(8,128)(2,1)S(1)}, bf16[128,1024]{1,0:T(8,128)(2,1)}, u32[]{:S(2)}) copy-start(bf16[128,1024]{1,0:T(8,128)(2,1)} %param.16) | copy-start | bytes 786436
  1.7 23.9 %collective-permute-start.2 = (bf16[128,256]{0,1:T(8,128)(2,1)S(1)}, bf16[128,256]{0,1:T(8,128)(2,1)S(1)}, u32[]{:S(2)}, u32[]{:S(2)}) collective-permute-start(bf16[128,256]{0,1:T(8,128)(2,1)S(1)} %copy.146), channel_id=1, source_target_pairs={{0,8},{2,10},{4,12},{6,14},{8,0},{10,2},{12,4},{14,6},{1,9},{3,11}... | collective-permute-start | bytes 196616 | tf_op jit(solution)/shard_map/ppermute | solution.py:16
  4.7 20.9 %collective-permute-start.1 = (bf16[128,256]{0,1:T(8,128)(2,1)S(1)}, bf16[128,256]{0,1:T(8,128)(2,1)S(1)}, u32[]{:S(2)}, u32[]{:S(2)}) collective-permute-start(bf16[128,256]{0,1:T(8,128)(2,1)S(1)} %copy.146), channel_id=1, source_target_pairs={{0,4},{2,6},{4,0},{6,2},{8,12},{10,14},{12,8},{14,10},{1,5},{3,7},... | collective-permute-start | bytes 196616 | tf_op jit(solution)/shard_map/ppermute | solution.py:16
  7.3 16.0 %collective-permute-start.4 = (bf16[128,256]{1,0:T(8,128)(2,1)}, bf16[128,256]{1,0:T(8,128)(2,1)S(1)}, u32[]{:S(2)}, u32[]{:S(2)}) collective-permute-start(bf16[128,256]{1,0:T(8,128)(2,1)} %param.18), channel_id=1, source_target_pairs={{0,4},{2,6},{4,0},{6,2},{8,12},{10,14},{12,8},{14,10},{1,5},{3,7},... | collective-permute-start | bytes 196616 | tf_op jit(solution)/shard_map/ppermute | solution.py:16
  7.6 17.8 %collective-permute-start.3 = (bf16[128,256]{1,0:T(8,128)(2,1)}, bf16[128,256]{1,0:T(8,128)(2,1)S(1)}, u32[]{:S(2)}, u32[]{:S(2)}) collective-permute-start(bf16[128,256]{1,0:T(8,128)(2,1)} %param.18), channel_id=1, source_target_pairs={{0,2},{2,0},{4,6},{6,4},{8,10},{10,8},{12,14},{14,12},{1,3},{3,1},... | collective-permute-start | bytes 196616 | tf_op jit(solution)/shard_map/ppermute | solution.py:16
  9.2 16.2 %collective-permute-start.5 = (bf16[128,256]{1,0:T(8,128)(2,1)}, bf16[128,256]{1,0:T(8,128)(2,1)S(1)}, u32[]{:S(2)}, u32[]{:S(2)}) collective-permute-start(bf16[128,256]{1,0:T(8,128)(2,1)} %param.18), channel_id=1, source_target_pairs={{0,8},{2,10},{4,12},{6,14},{8,0},{10,2},{12,4},{14,6},{1,9},{3,11}... | collective-permute-start | bytes 196616 | tf_op jit(solution)/shard_map/ppermute | solution.py:16
  9.7 24.4 %all-to-all-start = ((bf16[1,1,4,80,1024]{4,3,1,0,2:T(8,128)(2,1)}), bf16[1,1,4,80,1024]{4,3,1,0,2:T(8,128)(2,1)S(1)}, u32[]{:S(2)}, u32[]{:S(2)}) async-start(bf16[1,1,4,80,1024]{4,3,1,0,2:T(8,128)(2,1)} %bitcast.132), calls=%async_computation | async-start | bytes 1310720 | tf_op jit(solution)/shard_map/all_to_all | solution.py:109
  23.3 6.5 %collective-permute-start = (bf16[128,256]{0,1:T(8,128)(2,1)S(1)}, bf16[128,256]{0,1:T(8,128)(2,1)S(1)}, u32[]{:S(2)}, u32[]{:S(2)}) collective-permute-start(bf16[128,256]{0,1:T(8,128)(2,1)S(1)} %copy.146), channel_id=1, source_target_pairs={{0,2},{2,0},{4,6},{6,4},{8,10},{10,8},{12,14},{14,12},{1,3},{3,1},... | collective-permute-start | bytes 196616 | tf_op jit(solution)/shard_map/ppermute | solution.py:16
  35.3 1.9 %copy-start.2 = (bf16[128,1024]{1,0:T(8,128)(2,1)S(1)}, bf16[128,1024]{1,0:T(8,128)(2,1)}, u32[]{:S(2)}) copy-start(bf16[128,1024]{1,0:T(8,128)(2,1)} %param.19) | copy-start | bytes 786436
  35.3 4.6 %copy-start.5 = (f32[1024]{0:T(1024)S(1)}, f32[1024]{0:T(1024)}, u32[]{:S(2)}) copy-start(f32[1024]{0:T(1024)} %param.26) | copy-start | bytes 12292
  37.2 6.9 %copy-start.6 = (f32[64,64]{1,0:T(8,128)S(1)}, f32[64,64]{1,0:T(8,128)}, u32[]{:S(2)}) copy-start(f32[64,64]{1,0:T(8,128)} %param.25) | copy-start | bytes 49156
  52.9 25.5 %collective-permute-start.10 = (bf16[1,128,256]{2,1,0:T(8,128)(2,1)S(1)}, bf16[1,128,256]{2,1,0:T(8,128)(2,1)S(1)}, u32[]{:S(2)}, u32[]{:S(2)}) collective-permute-start(bf16[1,128,256]{2,1,0:T(8,128)(2,1)S(1)} %copy.175), channel_id=1, source_target_pairs={{0,4},{2,6},{4,0},{6,2},{8,12},{10,14},{12,8},{14,10},{1,5},{3,7},... | collective-permute-start | bytes 196616 | tf_op jit(solution)/shard_map/ppermute | solution.py:16
  53.8 26.2 %collective-permute-start.11 = (bf16[1,128,256]{2,1,0:T(8,128)(2,1)S(1)}, bf16[1,128,256]{2,1,0:T(8,128)(2,1)S(1)}, u32[]{:S(2)}, u32[]{:S(2)}) collective-permute-start(bf16[1,128,256]{2,1,0:T(8,128)(2,1)S(1)} %copy.176), channel_id=1, source_target_pairs={{0,8},{2,10},{4,12},{6,14},{8,0},{10,2},{12,4},{14,6},{1,9},{3,11}... | collective-permute-start | bytes 196616 | tf_op jit(solution)/shard_map/ppermute | solution.py:16
  55.3 24.7 %collective-permute-start.9 = (bf16[1,128,256]{2,1,0:T(8,128)(2,1)S(1)}, bf16[1,128,256]{2,1,0:T(8,128)(2,1)S(1)}, u32[]{:S(2)}, u32[]{:S(2)}) collective-permute-start(bf16[1,128,256]{2,1,0:T(8,128)(2,1)S(1)} %copy.173), channel_id=1, source_target_pairs={{0,2},{2,0},{4,6},{6,4},{8,10},{10,8},{12,14},{14,12},{1,3},{3,1},... | collective-permute-start | bytes 196616 | tf_op jit(solution)/shard_map/ppermute | solution.py:16
  60.6 24.9 %all-to-all-start.1 = ((bf16[1,4,1,80,1024]{4,3,2,0,1:T(8,128)(2,1)}), bf16[1,4,1,80,1024]{4,3,2,0,1:T(8,128)(2,1)S(1)}, u32[]{:S(2)}, u32[]{:S(2)}) async-start(bf16[1,4,1,80,1024]{4,3,2,0,1:T(8,128)(2,1)} %bitcast.43), calls=%async_computation.1 | async-start | bytes 1310720 | tf_op jit(solution)/shard_map/all_to_all | solution.py:197
  74.8 9.4 %collective-permute-start.7 = (bf16[1,128,256]{2,1,0:T(8,128)(2,1)S(1)}, bf16[1,128,256]{2,1,0:T(8,128)(2,1)S(1)}, u32[]{:S(2)}, u32[]{:S(2)}) collective-permute-start(bf16[1,128,256]{2,1,0:T(8,128)(2,1)S(1)} %copy.169), channel_id=1, source_target_pairs={{0,4},{2,6},{4,0},{6,2},{8,12},{10,14},{12,8},{14,10},{1,5},{3,7},... | collective-permute-start | bytes 196616 | tf_op jit(solution)/shard_map/ppermute | solution.py:16
  77.8 6.4 %collective-permute-start.8 = (bf16[1,128,256]{2,1,0:T(8,128)(2,1)S(1)}, bf16[1,128,256]{2,1,0:T(8,128)(2,1)S(1)}, u32[]{:S(2)}, u32[]{:S(2)}) collective-permute-start(bf16[1,128,256]{2,1,0:T(8,128)(2,1)S(1)} %copy.170), channel_id=1, source_target_pairs={{0,8},{2,10},{4,12},{6,14},{8,0},{10,2},{12,4},{14,6},{1,9},{3,11}... | collective-permute-start | bytes 196616 | tf_op jit(solution)/shard_map/ppermute | solution.py:16
  78.4 6.4 %collective-permute-start.6 = (bf16[1,128,256]{2,1,0:T(8,128)(2,1)S(1)}, bf16[1,128,256]{2,1,0:T(8,128)(2,1)S(1)}, u32[]{:S(2)}, u32[]{:S(2)}) collective-permute-start(bf16[1,128,256]{2,1,0:T(8,128)(2,1)S(1)} %copy.167), channel_id=1, source_target_pairs={{0,2},{2,0},{4,6},{6,4},{8,10},{10,8},{12,14},{14,12},{1,3},{3,1},... | collective-permute-start | bytes 196616 | tf_op jit(solution)/shard_map/ppermute | solution.py:16
where the time goes:
time: 86.8 us; the launch traced here: 86.3 us
  starting transfers between devices  26.5 us (31%)
  matrix products  18.9 us (22%)
  local copies, waits for them, and re-layouts  12.7 us (15%)
  other arithmetic  10.4 us (12%)
  waiting for transfers between devices  8.35 us (10%)
  blocking collectives  8.33 us (10%)
  between operations  1.07 us (1%)
    ppermute x12, starting transfers between devices, swapped(): lax.ppermute(array, axis, [(i, i ^ 1 << distance) for i in range(lax.axis...  19.1 us
    ppermute x12, waiting for transfers between devices, swapped(): lax.ppermute(array, axis, [(i, i ^ 1 << distance) for i in range(lax.axis...  8.34 us
    unnamed x19, local copies, waits for them, and re-layouts  4.31 us
    dot_general x1, matrix products, local(): jnp.einsum('rcnw,nrco->wro', grad_score, q_blocks[block_position], prefer...  4.24 us
    dot_general x1, matrix products, local(): jnp.einsum('kgqs,skd->qkgd', grad_score, key_set, preferred_element_type=...  4.23 us
    all_to_all x1, starting transfers between devices, local(): lax.all_to_all(expert_out, 'expert', split_axis=2, concat_axis=1, tiled=T...  3.86 us
    all_to_all x1, starting transfers between devices, local(): lax.all_to_all(buffer.reshape(1, experts, 1, capacity, -1), 'expert', spl...  3.48 us
    psum x1, blocking collectives, local(): lax.psum(jnp.dot(normed, head_weight, precision=HIGHEST_PRECISION), 'tens...  3.4 us
  transfers between devices with their start and end apart: 14, of which 3 were waited for; matrix products, arithmetic and copies ran while one was open for 35% of the time, Pallas kernels for 0%

commit v1 on v0

--- a/solution.py
+++ b/solution.py
@@ -124,7 +124,9 @@
     square_sum = lax.psum(jnp.sum(hidden * hidden, axis=1), "tensor")
     row_rms = jnp.sqrt(square_sum / D + EPSILON)
     normed = hidden / row_rms[:, None] * gain
-    logits = lax.psum(jnp.dot(normed, head_weight, precision=HIGHEST_PRECISION), "tensor")
+    logits = jnp.sum(
+        lax.all_gather(jnp.dot(normed, head_weight, precision=HIGHEST_PRECISION), "tensor"), axis=0
+    )
     turn_ends = jnp.cumsum(lengths)
     position = shard_id * tok_dev + jnp.arange(tok_dev, dtype=jnp.int32)
     turn_id = jnp.sum((turn_ends[None, :] <= position[:, None]).astype(jnp.int32), axis=1)

time: 86.8 us -> 85.2 us (0.982)
  blocking collectives: 8.33 us -> 6.78 us
    psum x1 -> x0, blocking collectives: 3.4 us -> none  [local(): lax.psum(jnp.dot(normed, head_weight, precision=HIGHEST_PRECISION), 'tens...]
    all_gather x0 -> x1, blocking collectives: none -> 1.85 us  [local(): lax.all_gather(jnp.dot(normed, head_weight, precision=HIGHEST_PRECISION),...]
where the time goes in v1:
time: 85.2 us; the launch traced here: 84.7 us
  starting transfers between devices  26.5 us (31%)
  matrix products  18.9 us (22%)
  local copies, waits for them, and re-layouts  12.8 us (15%)
  other arithmetic  10.5 us (12%)
  waiting for transfers between devices  8.16 us (10%)
  blocking collectives  6.78 us (8%)
  between operations  1.08 us (1%)
    ppermute x12, starting transfers between devices, swapped(): lax.ppermute(array, axis, [(i, i ^ 1 << distance) for i in range(lax.axis...  19.1 us
    ppermute x12, waiting for transfers between devices, swapped(): lax.ppermute(array, axis, [(i, i ^ 1 << distance) for i in range(lax.axis...  8.16 us
    unnamed x19, local copies, waits for them, and re-layouts  4.31 us
    dot_general x1, matrix products, local(): jnp.einsum('rcnw,nrco->wro', grad_score, q_blocks[block_position], prefer...  4.24 us
    dot_general x1, matrix products, local(): jnp.einsum('kgqs,skd->qkgd', grad_score, key_set, preferred_element_type=...  4.23 us
    all_to_all x1, starting transfers between devices, local(): lax.all_to_all(expert_out, 'expert', split_axis=2, concat_axis=1, tiled=T...  3.86 us
    all_to_all x1, starting transfers between devices, local(): lax.all_to_all(buffer.reshape(1, experts, 1, capacity, -1), 'expert', spl...  3.48 us
    dot_general x1, matrix products, local(): jnp.einsum('rcnw,nrco->wro', weight_rows, grad_out[block_position], prefe...  2.87 us
  transfers between devices with their start and end apart: 14, of which 3 were waited for; matrix products, arithmetic and copies ran while one was open for 35% of the time, Pallas kernels for 0%

profile of v1, /device:TPU:0, one launch (start us, length us, event | category | flops | bytes accessed | tf_op | source)
XLA Modules:
  0.0 84.7 jit_solution(6711943017318757392)
XLA Ops:
  0.7 1.0 %copy.146 = bf16[128,256]{0,1:T(8,128)(2,1)S(1)} copy(bf16[128,256]{1,0:T(8,128)(2,1)} %param.17) | data formatting | bytes 131072 | tf_op args[1]
  1.7 3.0 %collective-permute-start.2 = (bf16[128,256]{0,1:T(8,128)(2,1)S(1)}, bf16[128,256]{0,1:T(8,128)(2,1)S(1)}, u32[]{:S(2)}, u32[]{:S(2)}) collective-permute-start(bf16[128,256]{0,1:T(8,128)(2,1)S(1)} %copy.146), channel_id=1, source_target_pairs={{0,8},{2,10},{4,12},{6,14},{8,0},{10,2},{12,4},{14,6},{1,9},{3,11}... | collective-permute-start | bytes 196616 | tf_op jit(solution)/shard_map/ppermute | solution.py:16
  4.7 2.6 %collective-permute-start.1 = (bf16[128,256]{0,1:T(8,128)(2,1)S(1)}, bf16[128,256]{0,1:T(8,128)(2,1)S(1)}, u32[]{:S(2)}, u32[]{:S(2)}) collective-permute-start(bf16[128,256]{0,1:T(8,128)(2,1)S(1)} %copy.146), channel_id=1, source_target_pairs={{0,4},{2,6},{4,0},{6,2},{8,12},{10,14},{12,8},{14,10},{1,5},{3,7},... | collective-permute-start | bytes 196616 | tf_op jit(solution)/shard_map/ppermute | solution.py:16
  7.6 1.6 %collective-permute-start.3 = (bf16[128,256]{1,0:T(8,128)(2,1)}, bf16[128,256]{1,0:T(8,128)(2,1)S(1)}, u32[]{:S(2)}, u32[]{:S(2)}) collective-permute-start(bf16[128,256]{1,0:T(8,128)(2,1)} %param.18), channel_id=1, source_target_pairs={{0,2},{2,0},{4,6},{6,4},{8,10},{10,8},{12,14},{14,12},{1,3},{3,1},... | collective-permute-start | bytes 196616 | tf_op jit(solution)/shard_map/ppermute | solution.py:16
  9.7 3.9 %all-to-all-start = ((bf16[1,1,4,80,1024]{4,3,1,0,2:T(8,128)(2,1)}), bf16[1,1,4,80,1024]{4,3,1,0,2:T(8,128)(2,1)S(1)}, u32[]{:S(2)}, u32[]{:S(2)}) async-start(bf16[1,1,4,80,1024]{4,3,1,0,2:T(8,128)(2,1)} %bitcast.134), calls=%async_computation | async-start | bytes 1310720 | tf_op jit(solution)/shard_map/all_to_all | solution.py:109
  15.4 1.4 %constant_dynamic-slice_fusion.2 = (s32[1,1]{1,0:T(1,128)}, s32[1,1]{1,0:T(1,128)}, s32[1,1]{1,0:T(1,128)}) fusion(s32[1,8]{1,0:T(1,128)} %param.23, s32[]{:T(128)S(6)} %select_n.39, s32[]{:T(128)S(6)} %select_n.41, s32[]{:T(128)S(6)} %select_n.40), kind=kLoop, calls=%fused_computation.66 | loop fusion | bytes 36 | tf_op jit(solution)/shard_map/dynamic_slice | solution.py:90
  16.7 2.0 %add_compare_fusion = pred[4]{0:T(512)(128)(4,1)S(1)} fusion(s32[1]{0:T(128)} %bitcast.5, s32[1]{0:T(128)} %bitcast.4, s32[1]{0:T(128)} %bitcast.3, s32[1]{0:T(128)} %constant.90.clone.1), kind=kLoop, calls=%fused_computation.69 | loop fusion | flops 16 | bytes 20 | tf_op jit(solution)/shard_map/gt | solution.py:92
  21.0 1.2 %reduce-window.18 = s32[4,2,128]{2,1,0:T(2,128)S(1)} reduce-window(s32[4,2,128]{2,1,0:T(2,128)S(1)} %compare_convert_fusion, s32[]{:T(128)} %constant.91.clone.1), window={size=1x1x128 pad=0_0x0_0x127_0}, to_apply=%region_2.3 | reduce-window | flops 130048 | bytes 8196 | tf_op jit(solution)/shard_map/reduce-window
  23.3 2.1 %collective-permute-start = (bf16[128,256]{0,1:T(8,128)(2,1)S(1)}, bf16[128,256]{0,1:T(8,128)(2,1)S(1)}, u32[]{:S(2)}, u32[]{:S(2)}) collective-permute-start(bf16[128,256]{0,1:T(8,128)(2,1)S(1)} %copy.146), channel_id=1, source_target_pairs={{0,2},{2,0},{4,6},{6,4},{8,10},{10,8},{12,14},{14,12},{1,3},{3,1},... | collective-permute-start | bytes 196616 | tf_op jit(solution)/shard_map/ppermute | solution.py:16
  25.6 4.2 %collective-permute-done = bf16[128,256]{0,1:T(8,128)(2,1)S(1)} collective-permute-done((bf16[128,256]{0,1:T(8,128)(2,1)S(1)}, bf16[128,256]{0,1:T(8,128)(2,1)S(1)}, u32[]{:S(2)}, u32[]{:S(2)}) %collective-permute-start) | collective-permute-done | bytes 65568 | tf_op jit(solution)/shard_map/ppermute | solution.py:16
  29.8 2.2 %fusion.42 = (f32[2,4,128]{2,1,0:T(4,128)S(1)}, f32[2,4,128,512]{2,3,1,0:T(8,128)}) fusion(pred[512]{0:T(512)(128)(4,1)S(1)} %broadcast_bitcast_fusion, bf16[512,2,128,1]{0,2,3,1:T(8,128)(2,1)S(1)} %bitcast.140, bf16[128,2,4,128]{0,3,2,1:T(8,128)(2,1)S(1)} %bitcast.138), kind=kOutput, calls=%fused_computation.82 | convolution fusion | flops 136315392 | bytes 2626048 | tf_op jit(solution)/shard_map/sub | solution.py:26
  32.0 1.9 %fusion.20 = f32[2,128,4,128]{3,1,2,0:T(8,128)S(1)} fusion(bf16[512,2,128,1]{0,2,3,1:T(8,128)(2,1)S(1)} %bitcast.130, f32[2,4,128,512]{2,3,1,0:T(8,128)} %get-tuple-element.62, f32[2,4,128]{2,1,0:T(4,128)S(1)} %get-tuple-element.61), kind=kOutput, calls=%fused_computation.38 | convolution fusion | flops 135266304 | bytes 2887680 | tf_op jit(solution)/shard_map/kgqs,skd->qkgd/dot_general | solution.py:100
  34.2 1.2 %gather_fusion = bf16[256,1024]{1,0:T(8,128)(2,1)S(1)} fusion(bf16[320,1024]{1,0:T(8,128)(2,1)S(1)} %bitcast.128, s32[1024]{0:T(1024)S(1)} %pad_clamp_fusion), kind=kCustom, calls=%fused_computation | custom fusion | bytes 1049600 | tf_op jit(solution)/shard_map/jit(_take)/gather | solution.py:118
  35.6 1.7 %multiply_reduce_fusion = f32[128,1024]{1,0:T(8,128)S(1)} fusion(bf16[128,2,1024]{2,1,0:T(2,128)(2,1)S(1)} %gather.7, pred[128,2]{1,0:T(8,128)(4,1)S(1)} %copy.158, f32[128,2]{1,0:T(8,128)S(1)} %copy.152), kind=kLoop, calls=%fused_computation.21 | loop fusion | flops 917504 | bytes 1049856 | tf_op jit(solution)/shard_map/reduce_sum | solution.py:122
  37.4 2.5 %psum.14 = f32[128]{0:T(128)S(1)} all-reduce(f32[128]{0:T(128)S(1)} %get-tuple-element.50), channel_id=1, replica_groups=mesh['groups'=2,'context'=2,'expert'=4,'tensor'=2] {'tensor'}, use_global_device_ids=true, to_apply=%region_7.8 | all-reduce | flops 128 | bytes 1024 | tf_op jit(solution)/shard_map/psum | solution.py:124
  40.7 1.9 %all-gather = f32[256,64]{0,1:T(8,128)S(1)} all-gather(f32[128,64]{0,1:T(8,128)S(1)} %fusion.16), channel_id=2, replica_groups=mesh['groups'=2,'context'=2,'expert'=4,'tensor'=2] {'tensor'}, dimensions={0}, use_global_device_ids=true | all-gather | bytes 98304 | tf_op jit(solution)/shard_map/all_gather | solution.py:128
  43.6 2.5 %psum.15 = f32[128]{0:T(128)S(1)} all-reduce(f32[128]{0:T(128)S(1)} %get-tuple-element.63), channel_id=1, replica_groups=mesh['groups'=2,'context'=2,'expert'=4,'tensor'=2] {'tensor'}, use_global_device_ids=true, to_apply=%region_12.13 | all-reduce | flops 128 | bytes 1024 | tf_op jit(solution)/shard_map/psum | solution.py:139
  46.5 2.9 %fusion.44 = (bf16[512,2,128]{0,2,1:T(8,128)(2,1)S(1)}, f32[512,2,128]{0,2,1:T(8,128)}) fusion(bf16[128,2,4,128]{0,3,2,1:T(8,128)(2,1)S(1)} %bitcast.132, f32[2,4,128,512]{2,3,1,0:T(8,128)} %get-tuple-element.62, f32[2,4,128]{2,1,0:T(4,128)S(1)} %get-tuple-element.61), kind=kOutput, calls=%fused_computation.84 | convolution fusion | flops 135397376 | bytes 3149824 | tf_op jit(solution)/shard_map/rcnw,nrco->wro/dot_general | solution.py:157
  49.3 1.8 %fusion.45 = f32[2,512,128,4]{2,1,3,0:T(8,128)} fusion(bf16[512,2,128,1]{0,2,3,1:T(8,128)(2,1)S(1)} %bitcast.131, bf16[128,2,4,128]{0,3,2,1:T(8,128)(2,1)S(1)} %bitcast.133), kind=kOutput, calls=%fused_computation.85 | convolution fusion | flops 134217728 | bytes 2621440 | tf_op jit(solution)/shard_map/qkgd,skd->kgqs/dot_general | solution.py:154
  51.5 0.8 %collective-permute-start.10 = (bf16[1,128,256]{2,1,0:T(8,128)(2,1)S(1)}, bf16[1,128,256]{2,1,0:T(8,128)(2,1)S(1)}, u32[]{:S(2)}, u32[]{:S(2)}) collective-permute-start(bf16[1,128,256]{2,1,0:T(8,128)(2,1)S(1)} %copy.175), channel_id=1, source_target_pairs={{0,4},{2,6},{4,0},{6,2},{8,12},{10,14},{12,8},{14,10},{1,5},{3,7},... | collective-permute-start | bytes 196616 | tf_op jit(solution)/shard_map/ppermute | solution.py:16
  52.3 1.5 %collective-permute-start.11 = (bf16[1,128,256]{2,1,0:T(8,128)(2,1)S(1)}, bf16[1,128,256]{2,1,0:T(8,128)(2,1)S(1)}, u32[]{:S(2)}, u32[]{:S(2)}) collective-permute-start(bf16[1,128,256]{2,1,0:T(8,128)(2,1)S(1)} %copy.176), channel_id=1, source_target_pairs={{0,8},{2,10},{4,12},{6,14},{8,0},{10,2},{12,4},{14,6},{1,9},{3,11}... | collective-permute-start | bytes 196616 | tf_op jit(solution)/shard_map/ppermute | solution.py:16
  53.8 1.6 %collective-permute-start.9 = (bf16[1,128,256]{2,1,0:T(8,128)(2,1)S(1)}, bf16[1,128,256]{2,1,0:T(8,128)(2,1)S(1)}, u32[]{:S(2)}, u32[]{:S(2)}) collective-permute-start(bf16[1,128,256]{2,1,0:T(8,128)(2,1)S(1)} %copy.173), channel_id=1, source_target_pairs={{0,2},{2,0},{4,6},{6,4},{8,10},{10,8},{12,14},{14,12},{1,3},{3,1},... | collective-permute-start | bytes 196616 | tf_op jit(solution)/shard_map/ppermute | solution.py:16
  56.6 2.6 %scatter_custom_fusion = bf16[320,1024]{1,0:T(8,128)(2,1)} fusion(s32[256]{0:T(256)S(1)} %bitcast.151, f32[256,1024]{1,0:T(8,128)S(1)} %mul.133, f32[256]{0:T(256)S(1)} %mul.130, bf16[]{:T(256)} %constant.112.clone.1), kind=kCustom, calls=%fused_computation.28 | custom fusion | flops 524288 | bytes 1704962 | tf_op jit(solution)/shard_map/scatter | solution.py:197
  59.1 3.5 %all-to-all-start.1 = ((bf16[1,4,1,80,1024]{4,3,2,0,1:T(8,128)(2,1)}), bf16[1,4,1,80,1024]{4,3,2,0,1:T(8,128)(2,1)S(1)}, u32[]{:S(2)}, u32[]{:S(2)}) async-start(bf16[1,4,1,80,1024]{4,3,2,0,1:T(8,128)(2,1)} %bitcast.43), calls=%async_computation.1 | async-start | bytes 1310720 | tf_op jit(solution)/shard_map/all_to_all | solution.py:199
  62.6 4.2 %convolution_convert_fusion = bf16[2,128,4,128]{3,1,2,0:T(8,128)(2,1)S(1)} fusion(bf16[512,2,128,1]{0,2,3,1:T(8,128)(2,1)S(1)} %bitcast.141, f32[2,512,128,4]{2,1,3,0:T(8,128)} %fusion.45, f32[2,4,128,512]{2,3,1,0:T(8,128)} %get-tuple-element.62, f32[2,4,128]{2,1,0:T(4,128)S(1)} %get-tuple-element.61), kind=kOutput, calls=%fused_computation.17 | convolution fusion | flops 138020352 | bytes 4722688 | tf_op jit(solution)/shard_map/kgqs,skd->qkgd/dot_general | solution.py:162
  66.9 4.2 %fusion.43 = (bf16[512,2,128]{0,2,1:T(8,128)(2,1)S(1)}, f32[512,2,128]{0,2,1:T(8,128)S(1)}) fusion(bf16[128,2,4,128]{0,3,2,1:T(8,128)(2,1)S(1)} %bitcast.139, f32[2,512,128,4]{2,1,3,0:T(8,128)} %fusion.45, f32[2,4,128,512]{2,3,1,0:T(8,128)} %get-tuple-element.62, f32[2,4,128]{2,1,0:T(4,128)S(1)} %get-tuple-element.61), kind=kOutput, calls=%fused_computation.83 | convolution fusion | flops 138020352 | bytes 5246976 | tf_op jit(solution)/shard_map/rcnw,nrco->wro/dot_general | solution.py:166
  71.2 0.9 %slice.99 = f32[128,2,128]{0,2,1:T(8,128)S(1)} slice(f32[512,2,128]{0,2,1:T(8,128)} %get-tuple-element.68), slice={[0:128], [0:2], [0:128]} | slice | bytes 262144 | tf_op jit(solution)/shard_map/slice | solution.py:170
  72.4 0.9 %copy.178 = bf16[128,1024]{1,0:T(8,128)(2,1)} copy(bf16[128,1024]{0,1:T(8,128)(2,1)S(1)} %bitcast.142) | data formatting | bytes 524288
  73.4 2.9 %collective-permute-start.7 = (bf16[1,128,256]{2,1,0:T(8,128)(2,1)S(1)}, bf16[1,128,256]{2,1,0:T(8,128)(2,1)S(1)}, u32[]{:S(2)}, u32[]{:S(2)}) collective-permute-start(bf16[1,128,256]{2,1,0:T(8,128)(2,1)S(1)} %copy.169), channel_id=1, source_target_pairs={{0,4},{2,6},{4,0},{6,2},{8,12},{10,14},{12,8},{14,10},{1,5},{3,7},... | collective-permute-start | bytes 196616 | tf_op jit(solution)/shard_map/ppermute | solution.py:16
  77.0 1.5 %collective-permute-start.6 = (bf16[1,128,256]{2,1,0:T(8,128)(2,1)S(1)}, bf16[1,128,256]{2,1,0:T(8,128)(2,1)S(1)}, u32[]{:S(2)}, u32[]{:S(2)}) collective-permute-start(bf16[1,128,256]{2,1,0:T(8,128)(2,1)S(1)} %copy.167), channel_id=1, source_target_pairs={{0,2},{2,0},{4,6},{6,4},{8,10},{10,8},{12,14},{14,12},{1,3},{3,1},... | collective-permute-start | bytes 196616 | tf_op jit(solution)/shard_map/ppermute | solution.py:16
  79.2 3.4 %collective-permute-done.7 = bf16[1,128,256]{2,1,0:T(8,128)(2,1)S(1)} collective-permute-done((bf16[1,128,256]{2,1,0:T(8,128)(2,1)S(1)}, bf16[1,128,256]{2,1,0:T(8,128)(2,1)S(1)}, u32[]{:S(2)}, u32[]{:S(2)}) %collective-permute-start.7) | collective-permute-done | bytes 65568 | tf_op jit(solution)/shard_map/ppermute | solution.py:16
  83.9 0.8 copy.198
  (88 shorter events, 13.4 us)
Async XLA Ops:
  0.6 39.3 %copy-start = (f32[1024,64]{0,1:T(8,128)S(1)}, f32[1024,64]{0,1:T(8,128)}, u32[]{:S(2)}) copy-start(f32[1024,64]{0,1:T(8,128)} %param.27) | copy-start | bytes 786436
  0.6 24.8 %copy-start.3 = (bf16[128,256]{1,0:T(8,128)(2,1)S(1)}, bf16[128,256]{1,0:T(8,128)(2,1)}, u32[]{:S(2)}) copy-start(bf16[128,256]{1,0:T(8,128)(2,1)} %param.18) | copy-start | bytes 196612
  0.7 22.2 %copy-start.4 = (s32[128,2]{0,1:T(2,128)S(1)}, s32[128,2]{0,1:T(2,128)}, u32[]{:S(2)}) copy-start(s32[128,2]{0,1:T(2,128)} %param.21) | copy-start | bytes 3076
  0.7 22.3 %copy-start.1 = (bf16[128,1024]{1,0:T(8,128)(2,1)S(1)}, bf16[128,1024]{1,0:T(8,128)(2,1)}, u32[]{:S(2)}) copy-start(bf16[128,1024]{1,0:T(8,128)(2,1)} %param.16) | copy-start | bytes 786436
  1.7 23.9 %collective-permute-start.2 = (bf16[128,256]{0,1:T(8,128)(2,1)S(1)}, bf16[128,256]{0,1:T(8,128)(2,1)S(1)}, u32[]{:S(2)}, u32[]{:S(2)}) collective-permute-start(bf16[128,256]{0,1:T(8,128)(2,1)S(1)} %copy.146), channel_id=1, source_target_pairs={{0,8},{2,10},{4,12},{6,14},{8,0},{10,2},{12,4},{14,6},{1,9},{3,11}... | collective-permute-start | bytes 196616 | tf_op jit(solution)/shard_map/ppermute | solution.py:16
  4.7 20.9 %collective-permute-start.1 = (bf16[128,256]{0,1:T(8,128)(2,1)S(1)}, bf16[128,256]{0,1:T(8,128)(2,1)S(1)}, u32[]{:S(2)}, u32[]{:S(2)}) collective-permute-start(bf16[128,256]{0,1:T(8,128)(2,1)S(1)} %copy.146), channel_id=1, source_target_pairs={{0,4},{2,6},{4,0},{6,2},{8,12},{10,14},{12,8},{14,10},{1,5},{3,7},... | collective-permute-start | bytes 196616 | tf_op jit(solution)/shard_map/ppermute | solution.py:16
  7.3 16.0 %collective-permute-start.4 = (bf16[128,256]{1,0:T(8,128)(2,1)}, bf16[128,256]{1,0:T(8,128)(2,1)S(1)}, u32[]{:S(2)}, u32[]{:S(2)}) collective-permute-start(bf16[128,256]{1,0:T(8,128)(2,1)} %param.18), channel_id=1, source_target_pairs={{0,4},{2,6},{4,0},{6,2},{8,12},{10,14},{12,8},{14,10},{1,5},{3,7},... | collective-permute-start | bytes 196616 | tf_op jit(solution)/shard_map/ppermute | solution.py:16
  7.6 17.8 %collective-permute-start.3 = (bf16[128,256]{1,0:T(8,128)(2,1)}, bf16[128,256]{1,0:T(8,128)(2,1)S(1)}, u32[]{:S(2)}, u32[]{:S(2)}) collective-permute-start(bf16[128,256]{1,0:T(8,128)(2,1)} %param.18), channel_id=1, source_target_pairs={{0,2},{2,0},{4,6},{6,4},{8,10},{10,8},{12,14},{14,12},{1,3},{3,1},... | collective-permute-start | bytes 196616 | tf_op jit(solution)/shard_map/ppermute | solution.py:16
  9.2 16.2 %collective-permute-start.5 = (bf16[128,256]{1,0:T(8,128)(2,1)}, bf16[128,256]{1,0:T(8,128)(2,1)S(1)}, u32[]{:S(2)}, u32[]{:S(2)}) collective-permute-start(bf16[128,256]{1,0:T(8,128)(2,1)} %param.18), channel_id=1, source_target_pairs={{0,8},{2,10},{4,12},{6,14},{8,0},{10,2},{12,4},{14,6},{1,9},{3,11}... | collective-permute-start | bytes 196616 | tf_op jit(solution)/shard_map/ppermute | solution.py:16
  9.7 24.4 %all-to-all-start = ((bf16[1,1,4,80,1024]{4,3,1,0,2:T(8,128)(2,1)}), bf16[1,1,4,80,1024]{4,3,1,0,2:T(8,128)(2,1)S(1)}, u32[]{:S(2)}, u32[]{:S(2)}) async-start(bf16[1,1,4,80,1024]{4,3,1,0,2:T(8,128)(2,1)} %bitcast.134), calls=%async_computation | async-start | bytes 1310720 | tf_op jit(solution)/shard_map/all_to_all | solution.py:109
  23.3 6.5 %collective-permute-start = (bf16[128,256]{0,1:T(8,128)(2,1)S(1)}, bf16[128,256]{0,1:T(8,128)(2,1)S(1)}, u32[]{:S(2)}, u32[]{:S(2)}) collective-permute-start(bf16[128,256]{0,1:T(8,128)(2,1)S(1)} %copy.146), channel_id=1, source_target_pairs={{0,2},{2,0},{4,6},{6,4},{8,10},{10,8},{12,14},{14,12},{1,3},{3,1},... | collective-permute-start | bytes 196616 | tf_op jit(solution)/shard_map/ppermute | solution.py:16
  35.3 1.9 %copy-start.2 = (bf16[128,1024]{1,0:T(8,128)(2,1)S(1)}, bf16[128,1024]{1,0:T(8,128)(2,1)}, u32[]{:S(2)}) copy-start(bf16[128,1024]{1,0:T(8,128)(2,1)} %param.19) | copy-start | bytes 786436
  35.3 4.6 %copy-start.5 = (f32[1024]{0:T(1024)S(1)}, f32[1024]{0:T(1024)}, u32[]{:S(2)}) copy-start(f32[1024]{0:T(1024)} %param.26) | copy-start | bytes 12292
  37.2 5.4 %copy-start.6 = (f32[64,64]{1,0:T(8,128)S(1)}, f32[64,64]{1,0:T(8,128)}, u32[]{:S(2)}) copy-start(f32[64,64]{1,0:T(8,128)} %param.25) | copy-start | bytes 49156
  51.5 25.5 %collective-permute-start.10 = (bf16[1,128,256]{2,1,0:T(8,128)(2,1)S(1)}, bf16[1,128,256]{2,1,0:T(8,128)(2,1)S(1)}, u32[]{:S(2)}, u32[]{:S(2)}) collective-permute-start(bf16[1,128,256]{2,1,0:T(8,128)(2,1)S(1)} %copy.175), channel_id=1, source_target_pairs={{0,4},{2,6},{4,0},{6,2},{8,12},{10,14},{12,8},{14,10},{1,5},{3,7},... | collective-permute-start | bytes 196616 | tf_op jit(solution)/shard_map/ppermute | solution.py:16
  52.3 26.2 %collective-permute-start.11 = (bf16[1,128,256]{2,1,0:T(8,128)(2,1)S(1)}, bf16[1,128,256]{2,1,0:T(8,128)(2,1)S(1)}, u32[]{:S(2)}, u32[]{:S(2)}) collective-permute-start(bf16[1,128,256]{2,1,0:T(8,128)(2,1)S(1)} %copy.176), channel_id=1, source_target_pairs={{0,8},{2,10},{4,12},{6,14},{8,0},{10,2},{12,4},{14,6},{1,9},{3,11}... | collective-permute-start | bytes 196616 | tf_op jit(solution)/shard_map/ppermute | solution.py:16
  53.8 24.7 %collective-permute-start.9 = (bf16[1,128,256]{2,1,0:T(8,128)(2,1)S(1)}, bf16[1,128,256]{2,1,0:T(8,128)(2,1)S(1)}, u32[]{:S(2)}, u32[]{:S(2)}) collective-permute-start(bf16[1,128,256]{2,1,0:T(8,128)(2,1)S(1)} %copy.173), channel_id=1, source_target_pairs={{0,2},{2,0},{4,6},{6,4},{8,10},{10,8},{12,14},{14,12},{1,3},{3,1},... | collective-permute-start | bytes 196616 | tf_op jit(solution)/shard_map/ppermute | solution.py:16
  59.1 24.7 %all-to-all-start.1 = ((bf16[1,4,1,80,1024]{4,3,2,0,1:T(8,128)(2,1)}), bf16[1,4,1,80,1024]{4,3,2,0,1:T(8,128)(2,1)S(1)}, u32[]{:S(2)}, u32[]{:S(2)}) async-start(bf16[1,4,1,80,1024]{4,3,2,0,1:T(8,128)(2,1)} %bitcast.43), calls=%async_computation.1 | async-start | bytes 1310720 | tf_op jit(solution)/shard_map/all_to_all | solution.py:199
  73.4 9.2 %collective-permute-start.7 = (bf16[1,128,256]{2,1,0:T(8,128)(2,1)S(1)}, bf16[1,128,256]{2,1,0:T(8,128)(2,1)S(1)}, u32[]{:S(2)}, u32[]{:S(2)}) collective-permute-start(bf16[1,128,256]{2,1,0:T(8,128)(2,1)S(1)} %copy.169), channel_id=1, source_target_pairs={{0,4},{2,6},{4,0},{6,2},{8,12},{10,14},{12,8},{14,10},{1,5},{3,7},... | collective-permute-start | bytes 196616 | tf_op jit(solution)/shard_map/ppermute | solution.py:16
  76.3 6.3 %collective-permute-start.8 = (bf16[1,128,256]{2,1,0:T(8,128)(2,1)S(1)}, bf16[1,128,256]{2,1,0:T(8,128)(2,1)S(1)}, u32[]{:S(2)}, u32[]{:S(2)}) collective-permute-start(bf16[1,128,256]{2,1,0:T(8,128)(2,1)S(1)} %copy.170), channel_id=1, source_target_pairs={{0,8},{2,10},{4,12},{6,14},{8,0},{10,2},{12,4},{14,6},{1,9},{3,11}... | collective-permute-start | bytes 196616 | tf_op jit(solution)/shard_map/ppermute | solution.py:16
  77.0 6.2 %collective-permute-start.6 = (bf16[1,128,256]{2,1,0:T(8,128)(2,1)S(1)}, bf16[1,128,256]{2,1,0:T(8,128)(2,1)S(1)}, u32[]{:S(2)}, u32[]{:S(2)}) collective-permute-start(bf16[1,128,256]{2,1,0:T(8,128)(2,1)S(1)} %copy.167), channel_id=1, source_target_pairs={{0,2},{2,0},{4,6},{6,4},{8,10},{10,8},{12,14},{14,12},{1,3},{3,1},... | collective-permute-start | bytes 196616 | tf_op jit(solution)/shard_map/ppermute | solution.py:16
